TPU v7x, 32 devices: a whole 2x2x4 slice. The times are simulated.
32 devices in a mesh: row: 8 (over z, core), col: 4 (over y, x).
Axes of the slice: x: 2, y: 2, z: 4, core: 2. Of those that a mesh axis runs over, the one named last changes fastest.
Arguments:
- amplitudes: float32 [2048, 2048], P('row', 'col'), may hold values from -6 to 6
- factor: float32 [2048, 512], P('col'), may hold values from -1.2 to 1.2
- denominators: float32 [2048, 2048], P('row', 'col'), may hold values from 1 to 4
Outputs:
- new_amplitudes: float32 [2048, 2048], P('row', 'col')
All inputs are finite; a program needn't handle non-finite values.
Results may differ from a plain program's by a relative error of at most 0.0001.
Values sent between devices are 32-bit elements; how exact they have to be, the bound alone decides.
A program may use at most 64 MiB of HBM per device.

v0:
```python
import math

import jax
import jax.numpy as jnp
from jax import lax
from jax.sharding import PartitionSpec as P

ITERS = 2


def broadcast(value, axis, source):
    kept = jnp.where(lax.axis_index(axis) == source, value, 0).astype(value.dtype)
    return lax.psum(kept, axis)


def inner(left, right):
    return lax.dot_general(left, right, (((1,), (1,)), ((), ())), precision=lax.Precision.HIGHEST)


def local(amplitudes, factor, denominators):
    high = lax.Precision.HIGHEST
    rows = amplitudes.shape[0]
    cols = amplitudes.shape[1]
    nrow = lax.axis_size("row")
    ratio = nrow // lax.axis_size("col")
    here_row = lax.axis_index("row")
    here_col = lax.axis_index("col")
    scale = 1.0 / math.sqrt(rows * nrow)
    mine = lax.dynamic_slice_in_dim(factor, here_row % ratio * rows, rows, 0)
    factor_rows = broadcast(mine, "col", here_row // ratio)
    base = inner(factor_rows, factor)
    amp = amplitudes
    for step in range(ITERS):
        partial_value = jnp.dot(amp, factor, precision=high)
        y_rows = lax.psum(partial_value, "col") * scale
        offset = here_row - here_col * ratio
        is_owner = jnp.logical_and(offset >= 0, offset < ratio)
        place_at = jnp.clip(offset, 0, ratio - 1) * rows
        placed = lax.dynamic_update_slice_in_dim(
            jnp.zeros((cols, y_rows.shape[1]), jnp.float32), y_rows, place_at, 0
        )
        placed = jnp.where(is_owner, placed, jnp.zeros_like(placed))
        share = lax.psum_scatter(placed, "row", scatter_dimension=0, tiled=True)
        y_cols = lax.all_gather(share, "row", axis=0, tiled=True)
        result = base + inner(y_rows, y_cols) + inner(y_rows, factor) + inner(factor_rows, y_cols)
        amp = result / denominators
    return amp


def solution(mesh):
    return jax.shard_map(
        local,
        mesh=mesh,
        in_specs=(P("row", "col"), P("col", None), P("row", "col")),
        out_specs=P("row", "col"),
        check_vma=False,
    )
```

profile of v0, /device:TPU:7, one launch (start us, length us, event | category | flops | bytes accessed | tf_op | source)
XLA Modules:
  0.0 243.1 jit_solution(353994358076635832)
XLA Ops:
  6.5 0.0 copy-start
  6.5 0.0 all-reduce.6.cloned.1.call-start
  6.5 1.0 copy-done
  7.6 0.0 copy-start.1
  7.6 3.2 %fusion.15 = f32[256,512]{1,0:T(8,128)} fusion(f32[256,512]{1,0:T(8,128)S(1)} %copy-done, f32[512,512]{1,0:T(8,128)} %param.4), kind=kOutput, calls=%fused_computation.24 | convolution fusion | flops 805306368 | bytes 2097152 | tf_op jit(solution)/shard_map/dot_general | solution.py:34
  10.7 0.0 copy-done.1
  10.7 0.8 dynamic-slice_select_fusion
  11.6 0.0 all-reduce.6.cloned.1.call-update
  11.6 0.0 reduce-scatter.3.cloned.1.call-start
  11.7 53.1 %all-reduce.6.cloned.1.call-done = (f32[256,512]{1,0:T(8,128)}, f32[256,512]{1,0:T(8,128)}) async-done(((f32[256,512]{1,0:T(8,128)}, f32[256,512]{1,0:T(8,128)}), (f32[256,512]{1,0:T(8,128)}, f32[256,512]{1,0:T(8,128)})) %all-reduce.6.cloned.1.call-update) | async-done | bytes 1048592 | tf_op jit(solution)/shard_map/psum | solution.py:13
  64.8 0.0 copy-start.2
  64.8 1.1 broadcast.15.clone
  65.9 0.0 copy-done.2
  65.9 0.9 select_dynamic-update-slice_fusion.1
  66.7 0.0 copy-start.4
  66.7 0.0 reduce-scatter.3.cloned.1.call-update
  66.8 0.0 all-gather.3.cloned.1.call-start
  66.8 30.4 %reduce-scatter.3.cloned.1.call-done = f32[64,512]{1,0:T(8,128)} async-done(((f32[512,512]{1,0:T(8,128)}), f32[64,512]{1,0:T(8,128)}) %reduce-scatter.3.cloned.1.call-update) | async-done | bytes 131088 | tf_op jit(solution)/shard_map/reduce_scatter | solution.py:43
  97.2 0.0 all-gather.3.cloned.1.call-update
  97.2 0.0 all-reduce.4.cloned.1.call-start
  97.3 0.0 copy-done.4
  97.3 1.1 fusion.14
  98.4 24.3 %all-gather.3.cloned.1.call-done = f32[512,512]{1,0:T(8,128)} async-done(((f32[64,512]{1,0:T(8,128)}), f32[512,512]{1,0:T(8,128)}) %all-gather.3.cloned.1.call-update) | async-done | bytes 1048592 | tf_op jit(solution)/shard_map/all_gather | solution.py:44
  122.7 2.3 convolution_add_fusion.5
  125.0 0.0 copy-start.5
  125.0 0.0 copy-start.7
  125.0 1.1 convolution_add_fusion.4
  126.1 0.1 copy-done.5
  126.2 0.1 copy-done.7
  126.4 1.1 fusion
  127.4 1.8 fusion.16
  129.3 0.0 all-reduce.4.cloned.1.call-update
  129.3 0.0 reduce-scatter.5.cloned.1.call-start
  129.3 43.6 %all-reduce.4.cloned.1.call-done = f32[256,512]{1,0:T(8,128)} async-done(((f32[256,512]{1,0:T(8,128)}), f32[256,512]{1,0:T(8,128)}) %all-reduce.4.cloned.1.call-update) | async-done | bytes 524304 | tf_op jit(solution)/shard_map/psum | solution.py:35
  172.9 0.0 copy-start.3
  172.9 1.1 broadcast.15
  174.0 0.0 copy-done.3
  174.0 0.9 select_dynamic-update-slice_fusion
  174.9 0.0 reduce-scatter.5.cloned.1.call-update
  174.9 0.0 all-gather.5.cloned.1.call-start
  175.0 30.5 %reduce-scatter.5.cloned.1.call-done = f32[64,512]{1,0:T(8,128)} async-done(((f32[512,512]{1,0:T(8,128)}), f32[64,512]{1,0:T(8,128)}) %reduce-scatter.5.cloned.1.call-update) | async-done | bytes 131088 | tf_op jit(solution)/shard_map/reduce_scatter | solution.py:43
  205.5 0.0 all-gather.5.cloned.1.call-update
  205.6 25.2 %all-gather.5.cloned.1.call-done = f32[512,512]{1,0:T(8,128)} async-done(((f32[64,512]{1,0:T(8,128)}), f32[512,512]{1,0:T(8,128)}) %all-gather.5.cloned.1.call-update) | async-done | bytes 1048592 | tf_op jit(solution)/shard_map/all_gather | solution.py:44
  230.8 2.3 convolution_add_fusion.2
  233.1 0.0 copy-start.6
  233.1 0.0 copy-start.8
  233.1 1.1 convolution_add_fusion.1
  234.2 0.1 copy-done.6
  234.3 0.1 copy-done.8
  234.4 1.9 fusion.1
Async XLA Ops:
  6.5 1.0 copy-start
  6.5 58.2 %all-reduce.6.cloned.1.call-start = ((), (), s32[]{:S(2)}) async-start(), calls=%async_computation.7 | async-start | bytes 2097152 | tf_op jit(solution)/shard_map/psum | solution.py:13
  7.6 3.2 %copy-start.1 = (f32[512,512]{1,0:T(8,128)S(1)}, f32[512,512]{1,0:T(8,128)}, u32[]{:S(2)}) copy-start(f32[512,512]{1,0:T(8,128)} %param.4) | copy-start | bytes 3145732
  11.6 85.6 %reduce-scatter.3.cloned.1.call-start = ((), (), s32[]{:S(2)}) async-start(), calls=%async_computation.2 | async-start | bytes 1179648 | tf_op jit(solution)/shard_map/reduce_scatter | solution.py:43
  64.8 1.1 copy-start.2
  66.7 30.6 %copy-start.4 = (f32[256,512]{1,0:T(8,128)S(1)}, f32[256,512]{1,0:T(8,128)}, u32[]{:S(2)}) copy-start(f32[256,512]{1,0:T(8,128)} %get-tuple-element.5) | copy-start | bytes 1572868
  66.8 55.9 %all-gather.3.cloned.1.call-start = ((), (), s32[]{:S(2)}) async-start(), calls=%async_computation.3 | async-start | bytes 1179648 | tf_op jit(solution)/shard_map/all_gather | solution.py:44
  97.2 75.7 %all-reduce.4.cloned.1.call-start = ((), (), s32[]{:S(2)}) async-start(), calls=%async_computation.4 | async-start | bytes 1048576 | tf_op jit(solution)/shard_map/psum | solution.py:35
  125.0 1.2 copy-start.5
  125.0 1.3 copy-start.7
  129.3 76.2 %reduce-scatter.5.cloned.1.call-start = ((), (), s32[]{:S(2)}) async-start(), calls=%async_computation.5 | async-start | bytes 1179648 | tf_op jit(solution)/shard_map/reduce_scatter | solution.py:43
  172.9 1.1 copy-start.3
  174.9 55.8 %all-gather.5.cloned.1.call-start = ((), (), s32[]{:S(2)}) async-start(), calls=%async_computation.6 | async-start | bytes 1179648 | tf_op jit(solution)/shard_map/all_gather | solution.py:44
  233.1 1.2 copy-start.6
  233.1 1.3 copy-start.8
Sparse Core Ops, SparseCore 0:
  11.7 52.9 all-reduce.5
  67.0 30.1 reduce-scatter.2
  98.8 23.8 all-gather.2
  129.4 43.4 all-reduce.3
  175.1 30.4 reduce-scatter.4
  207.0 23.7 all-gather.4
where the time goes:
time: 245 us; the launch traced here: 243 us
  waiting for transfers between devices  207 us (84%)
  matrix products  15.7 us (6%)
  between operations  13.6 us (6%)
  local copies, waits for them, and re-layouts  3.81 us (2%)
  other arithmetic  2.56 us (1%)
    reduce_scatter x2, waiting for transfers between devices, local(): share = lax.psum_scatter(placed, 'row', scatter_dimension=0, tiled=True)  60.9 us
    psum x1, waiting for transfers between devices, broadcast(): return lax.psum(kept, axis)  53.1 us
    all_gather x2, waiting for transfers between devices, local(): y_cols = lax.all_gather(share, 'row', axis=0, tiled=True)  49.6 us
    psum x1, waiting for transfers between devices, local(): y_rows = lax.psum(partial_value, 'col') * scale  43.6 us
    dot_general x7, matrix products, inner(): lax.dot_general(left, right, (((1,), (1,)), ((), ())), precision=lax.Prec...  10.7 us
    dot_general x2, matrix products, local(): partial_value = jnp.dot(amp, factor, precision=high)  5 us
  transfers between devices with their start and end apart: 6, of which 6 were waited for; matrix products, arithmetic and copies ran while one was open for 0% of the time, Pallas kernels for 0%

commit v1 on v0

v1 whole, which is shorter than its diff:
```python
import functools
import math

import jax
import jax.numpy as jnp
from jax import lax
from jax.experimental import pallas as pl
from jax.experimental.pallas import tpu as pltpu
from jax.sharding import PartitionSpec as P

ITERS = 2
MESH = pl.DeviceIdType.MESH
NN = (((1,), (0,)), ((), ()))
NT = (((1,), (1,)), ((), ()))


def split(value):
    high = value.astype(jnp.bfloat16)
    return high, (value - high.astype(jnp.float32)).astype(jnp.bfloat16)


def product(left, right, dims):
    dot = functools.partial(lax.dot_general, dimension_numbers=dims, preferred_element_type=jnp.float32)
    return dot(left[0], right[0]) + (dot(left[0], right[1]) + dot(left[1], right[0]))


def kernel(nrow, ncol, scale, amp_hbm, fac_hbm, den_hbm, out_ref, amp, fac, den, fac_high, fac_low, part, got, zrow, zcol,
           load_sem, rs_send, rs_recv, ag_send, ag_recv, up_send, down_send, chain_recv, lane_send, lane_recv):
    rows, depth = part.shape[1] * part.shape[2], part.shape[3]
    piece = part.shape[2]
    lanes = nrow // ncol
    r = lax.axis_index("row")
    c = lax.axis_index("col")
    q = r // lanes
    k = r % lanes

    loads = [pltpu.make_async_copy(src, dst, load_sem.at[i])
             for i, (src, dst) in enumerate(((amp_hbm, amp), (fac_hbm, fac), (den_hbm, den)))]
    for load in loads:
        load.start()

    barrier = pltpu.get_barrier_semaphore()

    def greet(row, col):
        pl.semaphore_signal(barrier, inc=1, device_id=(row, col), device_id_type=MESH)

    others = [lax.rem(c + d, ncol) for d in range(1, ncol)]
    mates = [lax.rem(k + d, lanes) for d in range(1, lanes)]
    for j in others:
        greet(r, j)
    for m in mates:
        greet(q * lanes + m, c)

    @pl.when(q > 0)
    def _():
        greet(r - lanes, c)

    @pl.when(q < ncol - 1)
    def _():
        greet(r + lanes, c)

    def remote(src, dst, send, recv, row, col):
        return pltpu.make_async_remote_copy(src_ref=src, dst_ref=dst, send_sem=send, recv_sem=recv,
                                            device_id=(row, col), device_id_type=MESH)

    def reduce_copy(it, j):
        return remote(part.at[it, j], got.at[it, c], rs_send.at[it, j], rs_recv.at[it, c], r, j)

    def reduce_arrival(it, j):
        return remote(part.at[it, j], got.at[it, j], rs_send.at[it, j], rs_recv.at[it, j], r, j)

    def gather_copy(it, j):
        return remote(zrow.at[it, c], zrow.at[it, c], ag_send.at[it, j], ag_recv.at[it, c], r, j)

    def gather_arrival(it, j):
        return remote(zrow.at[it, j], zrow.at[it, j], ag_send.at[it, j], ag_recv.at[it, j], r, j)

    def up_copy(it, j):
        return remote(zcol.at[it, k, j], zcol.at[it, k, j], up_send.at[it, j], chain_recv.at[it, j], r + lanes, c)

    def down_copy(it, j):
        return remote(zcol.at[it, k, j], zcol.at[it, k, j], down_send.at[it, j], chain_recv.at[it, j], r - lanes, c)

    def lane_copy(it, m, j):
        return remote(zcol.at[it, k, j], zcol.at[it, k, j], lane_send.at[it, m, j], lane_recv.at[it, k, j], q * lanes + m, c)

    def lane_arrival(it, m, j):
        return remote(zcol.at[it, m, j], zcol.at[it, m, j], lane_send.at[it, m, j], lane_recv.at[it, m, j], q * lanes + m, c)

    goes_up = jnp.logical_and(q >= c, q < ncol - 1)
    goes_down = jnp.logical_and(q <= c, q > 0)

    loads[1].wait()
    fac_high[...], fac_low[...] = split(fac[...])
    loads[0].wait()
    loads[2].wait()

    for it in range(ITERS):
        value = product(split(amp[...]), (fac_high[...], fac_low[...]), NN) * scale
        here = fac[pl.ds(pl.multiple_of(k * rows, rows), rows), :]
        value = value + jnp.where(q == c, here, 0.0)
        part[it] = value.reshape(ncol, piece, depth)
        if it == 0:
            count = (ncol - 1) + (lanes - 1) + (q > 0).astype(jnp.int32) + (q < ncol - 1).astype(jnp.int32)
            pl.semaphore_wait(barrier, count)
        for j in others:
            reduce_copy(it, j).start()
        total = part[it, c]
        for j in others:
            reduce_arrival(it, j).wait_recv()
            total = total + got[it, j]
        zrow[it, c] = total

        for d, j in enumerate([c] + others):
            @pl.when(q == c)
            def _():
                if d > 0:
                    gather_arrival(it, j).wait_recv()
                zcol[it, k, j] = zrow[it, j]

            @pl.when(q != c)
            def _():
                up_copy(it, j).wait_recv()

            @pl.when(goes_up)
            def _():
                up_copy(it, j).start()

            @pl.when(goes_down)
            def _():
                down_copy(it, j).start()

            for m in mates:
                lane_copy(it, m, j).start()
            if d == 0:
                for jj in others:
                    gather_copy(it, jj).start()

        @pl.when(q != c)
        def _():
            for j in others:
                gather_arrival(it, j).wait_recv()

        for m in mates:
            for j in [c] + others:
                lane_arrival(it, m, j).wait_recv()
        left = split(zrow[it].reshape(rows, depth))
        right = split(zcol[it].reshape(lanes * rows, depth))
        result = product(left, right, NT) / den[...]
        if it < ITERS - 1:
            amp[...] = result
        else:
            out_ref[...] = result

    for it in range(ITERS):
        for j in others:
            reduce_copy(it, j).wait_send()
            gather_copy(it, j).wait_send()
        for j in range(ncol):
            @pl.when(goes_up)
            def _():
                up_copy(it, j).wait_send()

            @pl.when(goes_down)
            def _():
                down_copy(it, j).wait_send()

            for m in mates:
                lane_copy(it, m, j).wait_send()


def solution(mesh):
    nrow, ncol = mesh.shape["row"], mesh.shape["col"]
    lanes = nrow // ncol

    def local(amplitudes, factor, denominators):
        rows, cols = amplitudes.shape
        depth = factor.shape[1]
        piece = rows // ncol
        scale = 1.0 / math.sqrt(rows * nrow)
        dma = pltpu.SemaphoreType.DMA
        return pl.pallas_call(
            functools.partial(kernel, nrow, ncol, scale),
            out_shape=jax.ShapeDtypeStruct((rows, cols), jnp.float32),
            in_specs=[pl.BlockSpec(memory_space=pl.ANY)] * 3,
            out_specs=pl.BlockSpec(memory_space=pltpu.VMEM),
            scratch_shapes=[
                pltpu.VMEM((rows, cols), jnp.float32),
                pltpu.VMEM((cols, depth), jnp.float32),
                pltpu.VMEM((rows, cols), jnp.float32),
                pltpu.VMEM((cols, depth), jnp.bfloat16),
                pltpu.VMEM((cols, depth), jnp.bfloat16),
                pltpu.VMEM((ITERS, ncol, piece, depth), jnp.float32),
                pltpu.VMEM((ITERS, ncol, piece, depth), jnp.float32),
                pltpu.VMEM((ITERS, ncol, piece, depth), jnp.float32),
                pltpu.VMEM((ITERS, lanes, ncol, piece, depth), jnp.float32),
                dma((3,)),
                dma((ITERS, ncol)),
                dma((ITERS, ncol)),
                dma((ITERS, ncol)),
                dma((ITERS, ncol)),
                dma((ITERS, ncol)),
                dma((ITERS, ncol)),
                dma((ITERS, ncol)),
                dma((ITERS, lanes, ncol)),
                dma((ITERS, lanes, ncol)),
            ],
            compiler_params=pltpu.CompilerParams(
                collective_id=0, has_side_effects=True, vmem_limit_bytes=48 * 1024 * 1024
            ),
        )(amplitudes, factor, denominators)

    return jax.shard_map(
        local,
        mesh=mesh,
        in_specs=(P("row", "col"), P("col", None), P("row", "col")),
        out_specs=P("row", "col"),
        check_vma=False,
    )
```

time: 245 us -> 93.5 us (0.38)
  waiting for transfers between devices: 207 us -> 0 us
  Pallas kernels: 0 us -> 89.1 us
  matrix products: 15.7 us -> 0 us
  between operations: 13.6 us -> 0.01 us
  other arithmetic: 2.56 us -> 0 us
    psum x2 -> x0, waiting for transfers between devices: 96.7 us -> none  [the longest x1 53.1 us: broadcast(): return lax.psum(kept, axis)]
    pallas_call x0 -> x1, Pallas kernels: none -> 89.1 us  [local(): pl.pallas_call(functools.partial(kernel, nrow, ncol, scale), out_shape=ja...]
    reduce_scatter x2 -> x0, waiting for transfers between devices: 60.9 us -> none  [local(): share = lax.psum_scatter(placed, 'row', scatter_dimension=0, tiled=True)]
    all_gather x2 -> x0, waiting for transfers between devices: 49.6 us -> none  [local(): y_cols = lax.all_gather(share, 'row', axis=0, tiled=True)]
    dot_general x9 -> x0, matrix products: 15.7 us -> none  [the longest x7 10.7 us: inner(): lax.dot_general(left, right, (((1,), (1,)), ((), ())), precision=lax.Prec...]
    select_n x3 -> x0, other arithmetic: 2.56 us -> none  [the longest x2 1.73 us: local(): placed = jnp.where(is_owner, placed, jnp.zeros_like(placed))]
    unnamed x18 -> x7, local copies, waits for them, and re-layouts: 1.58 us -> 4.1 us
  transfers between devices with their start and end apart: 6 -> 0, of which waited for: 6 -> 0; matrix products, arithmetic and copies ran while one was open for 0% -> 0% of each run, Pallas kernels for 0% -> 0%
where the time goes in v1:
time: 93.5 us; the launch traced here: 93.2 us
  Pallas kernels  89.1 us (95%)
  local copies, waits for them, and re-layouts  4.1 us (4%)
    pallas_call x1, Pallas kernels, local(): pl.pallas_call(functools.partial(kernel, nrow, ncol, scale), out_shape=ja...  89.1 us
    unnamed x7, local copies, waits for them, and re-layouts  4.1 us

profile of v1, /device:TPU:7, one launch (start us, length us, event | category | flops | bytes accessed | tf_op | source)
XLA Modules:
  0.0 93.2 jit_solution(16534440418955385483)
XLA Ops:
  0.0 0.0 copy-start
  0.0 1.2 %copy-done = f32[512,512]{1,0:T(8,128)S(1)} copy-done((f32[512,512]{1,0:T(8,128)S(1)}, f32[512,512]{1,0:T(8,128)}, u32[]{:S(2)}) %copy-start) | copy-done | bytes 1048600
  1.2 0.0 copy-start.1
  1.2 1.0 %copy-done.1 = f32[256,512]{1,0:T(8,128)S(1)} copy-done((f32[256,512]{1,0:T(8,128)S(1)}, f32[256,512]{1,0:T(8,128)}, u32[]{:S(2)}) %copy-start.1) | copy-done | bytes 524312
  2.3 0.0 copy-start.2
  2.3 1.0 %copy-done.2 = f32[256,512]{1,0:T(8,128)S(1)} copy-done((f32[256,512]{1,0:T(8,128)S(1)}, f32[256,512]{1,0:T(8,128)}, u32[]{:S(2)}) %copy-start.2) | copy-done | bytes 524312
  3.3 89.1 %shard_map.37 = f32[256,512]{1,0:T(8,128)S(1)} custom-call(f32[256,512]{1,0:T(8,128)S(1)} %copy-done.1, f32[512,512]{1,0:T(8,128)S(1)} %copy-done, f32[256,512]{1,0:T(8,128)S(1)} %copy-done.2), custom_call_target="tpu_custom_call" | custom-call | tf_op jit(solution)/shard_map/pallas_call | solution.py:182
  92.4 0.8 copy.5
Async XLA Ops:
  0.0 1.2 %copy-start = (f32[512,512]{1,0:T(8,128)S(1)}, f32[512,512]{1,0:T(8,128)}, u32[]{:S(2)}) copy-start(f32[512,512]{1,0:T(8,128)} %fac_hbm.1) | copy-start | bytes 3145732
  1.2 1.0 %copy-start.1 = (f32[256,512]{1,0:T(8,128)S(1)}, f32[256,512]{1,0:T(8,128)}, u32[]{:S(2)}) copy-start(f32[256,512]{1,0:T(8,128)} %amp_hbm.1) | copy-start | bytes 1572868
  2.3 1.0 %copy-start.2 = (f32[256,512]{1,0:T(8,128)S(1)}, f32[256,512]{1,0:T(8,128)}, u32[]{:S(2)}) copy-start(f32[256,512]{1,0:T(8,128)} %den_hbm.1) | copy-start | bytes 1572868

commit v2 on v1

v2 whole, which is shorter than its diff:
```python
import functools
import math

import jax
import jax.numpy as jnp
from jax import lax
from jax.experimental import pallas as pl
from jax.experimental.pallas import tpu as pltpu
from jax.sharding import PartitionSpec as P

ITERS = 2
GROUPS = 4
OWN_LAG = 1
FAR_LAG = 4
MESH = pl.DeviceIdType.MESH
NN = (((1,), (0,)), ((), ()))
NT = (((1,), (1,)), ((), ()))


def split(value):
    high = value.astype(jnp.bfloat16)
    return high, (value - high.astype(jnp.float32)).astype(jnp.bfloat16)


def product(left, right, dims):
    dot = functools.partial(lax.dot_general, dimension_numbers=dims, preferred_element_type=jnp.float32)
    return dot(left[0], right[0]) + (dot(left[0], right[1]) + dot(left[1], right[0]))


def kernel(nrow, ncol, scale, amp_hbm, fac_hbm, den_hbm, out_ref, amp, fac, den, fac_high, fac_low, part, got, zrow, zcol,
           load_sem, rs_send, rs_recv, ag_send, ag_recv, up_send, down_send, chain_recv, lane_send, lane_recv):
    groups, piece, depth = part.shape[2:]
    rows = ncol * groups * piece
    lanes = nrow // ncol
    r = lax.axis_index("row")
    c = lax.axis_index("col")
    q = r // lanes
    k = r % lanes

    loads = [pltpu.make_async_copy(src, dst, load_sem.at[i])
             for i, (src, dst) in enumerate(((amp_hbm, amp), (fac_hbm, fac), (den_hbm, den)))]
    for load in loads:
        load.start()

    barrier = pltpu.get_barrier_semaphore()

    def greet(row, col):
        pl.semaphore_signal(barrier, inc=1, device_id=(row, col), device_id_type=MESH)

    others = [lax.rem(c + d, ncol) for d in range(1, ncol)]
    mates = [lax.rem(k + d, lanes) for d in range(1, lanes)]
    for j in others:
        greet(r, j)
    for m in mates:
        greet(q * lanes + m, c)

    @pl.when(q > 0)
    def _():
        greet(r - lanes, c)

    @pl.when(q < ncol - 1)
    def _():
        greet(r + lanes, c)

    def remote(src, dst, send, recv, row, col):
        return pltpu.make_async_remote_copy(src_ref=src, dst_ref=dst, send_sem=send, recv_sem=recv,
                                            device_id=(row, col), device_id_type=MESH)

    def reduce_copy(it, j, g):
        return remote(part.at[it, j, g], got.at[it, c, g], rs_send.at[it, j, g], rs_recv.at[it, c, g], r, j)

    def reduce_arrival(it, j, g):
        return remote(part.at[it, j, g], got.at[it, j, g], rs_send.at[it, j, g], rs_recv.at[it, j, g], r, j)

    def gather_copy(it, j, g):
        return remote(zrow.at[it, c, g], zrow.at[it, c, g], ag_send.at[it, j, g], ag_recv.at[it, c, g], r, j)

    def gather_arrival(it, j, g):
        return remote(zrow.at[it, j, g], zrow.at[it, j, g], ag_send.at[it, j, g], ag_recv.at[it, j, g], r, j)

    def up_copy(it, j, g):
        return remote(zcol.at[it, k, j, g], zcol.at[it, k, j, g], up_send.at[it, j, g], chain_recv.at[it, j, g], r + lanes, c)

    def down_copy(it, j, g):
        return remote(zcol.at[it, k, j, g], zcol.at[it, k, j, g], down_send.at[it, j, g], chain_recv.at[it, j, g], r - lanes, c)

    def lane_copy(it, m, j, g):
        return remote(zcol.at[it, k, j, g], zcol.at[it, k, j, g], lane_send.at[it, m, j, g], lane_recv.at[it, k, j, g], q * lanes + m, c)

    def lane_arrival(it, m, j, g):
        return remote(zcol.at[it, m, j, g], zcol.at[it, m, j, g], lane_send.at[it, m, j, g], lane_recv.at[it, m, j, g], q * lanes + m, c)

    goes_up = jnp.logical_and(q >= c, q < ncol - 1)
    goes_down = jnp.logical_and(q <= c, q > 0)

    loads[1].wait()
    fac_high[...], fac_low[...] = split(fac[...])
    loads[0].wait()
    loads[2].wait()

    for it in range(ITERS):
        value = product(split(amp[...]), (fac_high[...], fac_low[...]), NN) * scale
        here = fac[pl.ds(pl.multiple_of(k * rows, rows), rows), :]
        value = value + jnp.where(q == c, here, 0.0)
        part[it] = value.reshape(ncol, groups, piece, depth)
        if it == 0:
            count = (ncol - 1) + (lanes - 1) + (q > 0).astype(jnp.int32) + (q < ncol - 1).astype(jnp.int32)
            pl.semaphore_wait(barrier, count)
        for g in range(groups):
            for j in others:
                reduce_copy(it, j, g).start()

        def own(g):
            total = part[it, c, g]
            for j in others:
                reduce_arrival(it, j, g).wait_recv()
                total = total + got[it, j, g]
            zrow[it, c, g] = total

            @pl.when(q == c)
            def _():
                pass_on(c, g)

            for j in others:
                gather_copy(it, j, g).start()

        def pass_on(j, g):
            @pl.when(q == c)
            def _():
                zcol[it, k, j, g] = zrow[it, j, g]

            @pl.when(goes_up)
            def _():
                up_copy(it, j, g).start()

            @pl.when(goes_down)
            def _():
                down_copy(it, j, g).start()

            for m in mates:
                lane_copy(it, m, j, g).start()

        def from_plane(g):
            for j in others:
                gather_arrival(it, j, g).wait_recv()
                pass_on(j, g)

        def from_chain(g):
            for j in [c] + others:
                up_copy(it, j, g).wait_recv()
                pass_on(j, g)

        for step in range(groups + max(OWN_LAG, FAR_LAG)):
            if step < groups:
                own(step)
            if 0 <= step - OWN_LAG < groups:
                pl.when(q == c)(functools.partial(from_plane, step - OWN_LAG))
            if 0 <= step - FAR_LAG < groups:
                pl.when(q != c)(functools.partial(from_chain, step - FAR_LAG))

        @pl.when(q != c)
        def _():
            for g in range(groups):
                for j in others:
                    gather_arrival(it, j, g).wait_recv()

        for g in range(groups):
            for m in mates:
                for j in [c] + others:
                    lane_arrival(it, m, j, g).wait_recv()
        left = split(zrow[it].reshape(rows, depth))
        right = split(zcol[it].reshape(lanes * rows, depth))
        result = product(left, right, NT) / den[...]
        if it < ITERS - 1:
            amp[...] = result
        else:
            out_ref[...] = result

    for it in range(ITERS):
        for g in range(groups):
            for j in others:
                reduce_copy(it, j, g).wait_send()
                gather_copy(it, j, g).wait_send()
            for j in range(ncol):
                @pl.when(goes_up)
                def _():
                    up_copy(it, j, g).wait_send()

                @pl.when(goes_down)
                def _():
                    down_copy(it, j, g).wait_send()

                for m in mates:
                    lane_copy(it, m, j, g).wait_send()


def solution(mesh):
    nrow, ncol = mesh.shape["row"], mesh.shape["col"]
    lanes = nrow // ncol

    def local(amplitudes, factor, denominators):
        rows, cols = amplitudes.shape
        depth = factor.shape[1]
        groups = math.gcd(GROUPS, rows // ncol // 16)
        piece = rows // ncol // groups
        scale = 1.0 / math.sqrt(rows * nrow)
        dma = pltpu.SemaphoreType.DMA
        return pl.pallas_call(
            functools.partial(kernel, nrow, ncol, scale),
            out_shape=jax.ShapeDtypeStruct((rows, cols), jnp.float32),
            in_specs=[pl.BlockSpec(memory_space=pltpu.HBM)] * 3,
            out_specs=pl.BlockSpec(memory_space=pltpu.VMEM),
            scratch_shapes=[
                pltpu.VMEM((rows, cols), jnp.float32),
                pltpu.VMEM((cols, depth), jnp.float32),
                pltpu.VMEM((rows, cols), jnp.float32),
                pltpu.VMEM((cols, depth), jnp.bfloat16),
                pltpu.VMEM((cols, depth), jnp.bfloat16),
                pltpu.VMEM((ITERS, ncol, groups, piece, depth), jnp.float32),
                pltpu.VMEM((ITERS, ncol, groups, piece, depth), jnp.float32),
                pltpu.VMEM((ITERS, ncol, groups, piece, depth), jnp.float32),
                pltpu.VMEM((ITERS, lanes, ncol, groups, piece, depth), jnp.float32),
                dma((3,)),
                dma((ITERS, ncol, groups)),
                dma((ITERS, ncol, groups)),
                dma((ITERS, ncol, groups)),
                dma((ITERS, ncol, groups)),
                dma((ITERS, ncol, groups)),
                dma((ITERS, ncol, groups)),
                dma((ITERS, ncol, groups)),
                dma((ITERS, lanes, ncol, groups)),
                dma((ITERS, lanes, ncol, groups)),
            ],
            compiler_params=pltpu.CompilerParams(
                collective_id=0, has_side_effects=True, vmem_limit_bytes=48 * 1024 * 1024
            ),
        )(amplitudes, factor, denominators)

    return jax.shard_map(
        local,
        mesh=mesh,
        in_specs=(P("row", "col"), P("col", None), P("row", "col")),
        out_specs=P("row", "col"),
        check_vma=False,
    )
```

time: 93.5 us -> 66.2 us (0.71)
  Pallas kernels: 89.1 us -> 61.8 us
    pallas_call x1, Pallas kernels: 89.1 us -> 61.8 us  [local(): pl.pallas_call(functools.partial(kernel, nrow, ncol, scale), out_shape=ja...]
where the time goes in v2:
time: 66.2 us; the launch traced here: 66 us
  Pallas kernels  61.8 us (93%)
  local copies, waits for them, and re-layouts  4.1 us (6%)
    pallas_call x1, Pallas kernels, local(): pl.pallas_call(functools.partial(kernel, nrow, ncol, scale), out_shape=ja...  61.8 us
    unnamed x7, local copies, waits for them, and re-layouts  4.1 us

profile of v2, /device:TPU:7, one launch (start us, length us, event | category | flops | bytes accessed | tf_op | source)
XLA Modules:
  0.0 66.0 jit_solution(4383239690880501358)
XLA Ops:
  0.0 0.0 copy-start
  0.0 1.2 %copy-done = f32[512,512]{1,0:T(8,128)S(1)} copy-done((f32[512,512]{1,0:T(8,128)S(1)}, f32[512,512]{1,0:T(8,128)}, u32[]{:S(2)}) %copy-start) | copy-done | bytes 1048600
  1.2 0.0 copy-start.1
  1.2 1.0 %copy-done.1 = f32[256,512]{1,0:T(8,128)S(1)} copy-done((f32[256,512]{1,0:T(8,128)S(1)}, f32[256,512]{1,0:T(8,128)}, u32[]{:S(2)}) %copy-start.1) | copy-done | bytes 524312
  2.3 0.0 copy-start.2
  2.3 1.0 %copy-done.2 = f32[256,512]{1,0:T(8,128)S(1)} copy-done((f32[256,512]{1,0:T(8,128)S(1)}, f32[256,512]{1,0:T(8,128)}, u32[]{:S(2)}) %copy-start.2) | copy-done | bytes 524312
  3.3 61.8 %shard_map.37 = f32[256,512]{1,0:T(8,128)S(1)} custom-call(f32[256,512]{1,0:T(8,128)S(1)} %copy-done.1, f32[512,512]{1,0:T(8,128)S(1)} %copy-done, f32[256,512]{1,0:T(8,128)S(1)} %copy-done.2), custom_call_target="tpu_custom_call" | custom-call | tf_op jit(solution)/shard_map/pallas_call | solution.py:208
  65.2 0.8 %copy.5 = f32[256,512]{1,0:T(8,128)} copy(f32[256,512]{1,0:T(8,128)S(1)} %shard_map.37) | data formatting | bytes 1048576
Async XLA Ops:
  0.0 1.2 %copy-start = (f32[512,512]{1,0:T(8,128)S(1)}, f32[512,512]{1,0:T(8,128)}, u32[]{:S(2)}) copy-start(f32[512,512]{1,0:T(8,128)} %fac_hbm.1) | copy-start | bytes 3145732
  1.2 1.0 %copy-start.1 = (f32[256,512]{1,0:T(8,128)S(1)}, f32[256,512]{1,0:T(8,128)}, u32[]{:S(2)}) copy-start(f32[256,512]{1,0:T(8,128)} %amp_hbm.1) | copy-start | bytes 1572868
  2.3 1.0 %copy-start.2 = (f32[256,512]{1,0:T(8,128)S(1)}, f32[256,512]{1,0:T(8,128)}, u32[]{:S(2)}) copy-start(f32[256,512]{1,0:T(8,128)} %den_hbm.1) | copy-start | bytes 1572868

commit v3 on v2

--- a/solution.py
+++ b/solution.py
@@ -122,7 +122,12 @@
                 pass_on(c, g)
 
             for j in others:
-                gather_copy(it, j, g).start()
+                pl.when(j == q)(gather_copy(it, j, g).start)
+
+        def rest():
+            for g in range(groups):
+                for j in others:
+                    pl.when(j != q)(gather_copy(it, j, g).start)
 
         def pass_on(j, g):
             @pl.when(q == c)
@@ -153,6 +158,8 @@
         for step in range(groups + max(OWN_LAG, FAR_LAG)):
             if step < groups:
                 own(step)
+            if step == groups - 1:
+                rest()
             if 0 <= step - OWN_LAG < groups:
                 pl.when(q == c)(functools.partial(from_plane, step - OWN_LAG))
             if 0 <= step - FAR_LAG < groups:

time: 66.2 us -> 65.2 us (0.985)
  Pallas kernels: 61.8 us -> 60.2 us
    pallas_call x1, Pallas kernels: 61.8 us -> 60.2 us  [local(): pl.pallas_call(functools.partial(kernel, nrow, ncol, scale), out_shape=ja...]
where the time goes in v3:
time: 65.2 us; the launch traced here: 64.3 us
  Pallas kernels  60.2 us (92%)
  local copies, waits for them, and re-layouts  4.1 us (6%)
    pallas_call x1, Pallas kernels, local(): pl.pallas_call(functools.partial(kernel, nrow, ncol, scale), out_shape=ja...  60.2 us
    unnamed x7, local copies, waits for them, and re-layouts  4.1 us

profile of v3, /device:TPU:7, one launch (start us, length us, event | category | flops | bytes accessed | tf_op | source)
XLA Modules:
  0.0 64.3 jit_solution(4649224956365220734)
XLA Ops:
  0.0 0.0 copy-start
  0.0 1.2 %copy-done = f32[512,512]{1,0:T(8,128)S(1)} copy-done((f32[512,512]{1,0:T(8,128)S(1)}, f32[512,512]{1,0:T(8,128)}, u32[]{:S(2)}) %copy-start) | copy-done | bytes 1048600
  1.2 0.0 copy-start.1
  1.2 1.0 %copy-done.1 = f32[256,512]{1,0:T(8,128)S(1)} copy-done((f32[256,512]{1,0:T(8,128)S(1)}, f32[256,512]{1,0:T(8,128)}, u32[]{:S(2)}) %copy-start.1) | copy-done | bytes 524312
  2.3 0.0 copy-start.2
  2.3 1.0 %copy-done.2 = f32[256,512]{1,0:T(8,128)S(1)} copy-done((f32[256,512]{1,0:T(8,128)S(1)}, f32[256,512]{1,0:T(8,128)}, u32[]{:S(2)}) %copy-start.2) | copy-done | bytes 524312
  3.3 60.2 %shard_map.37 = f32[256,512]{1,0:T(8,128)S(1)} custom-call(f32[256,512]{1,0:T(8,128)S(1)} %copy-done.1, f32[512,512]{1,0:T(8,128)S(1)} %copy-done, f32[256,512]{1,0:T(8,128)S(1)} %copy-done.2), custom_call_target="tpu_custom_call" | custom-call | tf_op jit(solution)/shard_map/pallas_call | solution.py:215
  63.5 0.8 %copy.5 = f32[256,512]{1,0:T(8,128)} copy(f32[256,512]{1,0:T(8,128)S(1)} %shard_map.37) | data formatting | bytes 1048576
Async XLA Ops:
  0.0 1.2 %copy-start = (f32[512,512]{1,0:T(8,128)S(1)}, f32[512,512]{1,0:T(8,128)}, u32[]{:S(2)}) copy-start(f32[512,512]{1,0:T(8,128)} %fac_hbm.1) | copy-start | bytes 3145732
  1.2 1.0 %copy-start.1 = (f32[256,512]{1,0:T(8,128)S(1)}, f32[256,512]{1,0:T(8,128)}, u32[]{:S(2)}) copy-start(f32[256,512]{1,0:T(8,128)} %amp_hbm.1) | copy-start | bytes 1572868
  2.3 1.0 %copy-start.2 = (f32[256,512]{1,0:T(8,128)S(1)}, f32[256,512]{1,0:T(8,128)}, u32[]{:S(2)}) copy-start(f32[256,512]{1,0:T(8,128)} %den_hbm.1) | copy-start | bytes 1572868
